TPU v7x, 32 devices: a whole 2x2x4 slice. The times are simulated.
32 devices in a mesh: row: 16 (over z, x, core), col: 2 (over y).
Axes of the slice: x: 2, y: 2, z: 4, core: 2. Of those that a mesh axis runs over, the one named last changes fastest.
Arguments:
- corr: float32 [2, 8192, 8192], P(None, 'row', 'col'), may hold values from -6 to 6
- slope_prev: float32 [2, 8192, 8192], P(None, 'row', 'col'), may hold values from -6 to 6
- kappa: float32 [8192], replicated, may hold values from 0.05 to 0.2
- detuning: float32 [8192], replicated, may hold values from -1 to 1
- pump: float32 [8192], replicated, may hold values from 0.5 to 2
- round_trip: float32 [2], replicated, may hold values from -0.6 to 0.6
Outputs:
- slope: float32 [2, 8192, 8192], P(None, 'row', 'col')
All inputs are finite; a program needn't handle non-finite values.
Results may differ from a plain program's by a relative error of at most 0.00005.
Values sent between devices are 32-bit elements; how exact they have to be, the bound alone decides.
A program may use at most 256 MiB of HBM per device.

v0:
```python
import jax
import jax.numpy as jnp
from jax import lax
from jax.sharding import PartitionSpec as P


def lower_table(width):
    above = lax.broadcasted_iota(jnp.int32, (width, width), 0)
    beside = lax.broadcasted_iota(jnp.int32, (width, width), 1)
    return (above > beside).astype(jnp.float32)


def rows_prefix(part):
    count = part.shape[1]
    width = min(128, count)
    blocks = part.reshape(2, count // width, width, part.shape[2])
    within = jnp.einsum(
        "ij,pbjc->pbic", lower_table(width), blocks, precision=lax.Precision.HIGHEST
    )
    sums = jnp.sum(blocks, axis=2)
    earlier = jnp.cumsum(sums, axis=1) - sums
    return ((within + earlier[:, :, None, :]).reshape(part.shape), jnp.sum(sums, axis=1))


def cols_prefix(part):
    count = part.shape[2]
    width = min(128, count)
    blocks = part.reshape(2, part.shape[1], count // width, width)
    within = jnp.einsum(
        "prbj,ij->prbi", blocks, lower_table(width), precision=lax.Precision.HIGHEST
    )
    sums = jnp.sum(blocks, axis=3)
    earlier = jnp.cumsum(sums, axis=2) - sums
    return ((within + earlier[:, :, :, None]).reshape(part.shape), jnp.sum(sums, axis=2))


def lower_devices(pieces, own_index):
    marks = lax.broadcasted_iota(jnp.int32, (pieces.shape[0], 1, 1), 0) < own_index
    return jnp.sum(jnp.where(marks, pieces, 0.0), axis=0)


def higher_devices(pieces, own_index):
    marks = lax.broadcasted_iota(jnp.int32, (pieces.shape[0], 1, 1), 0) > own_index
    return jnp.sum(jnp.where(marks, pieces, 0.0), axis=0)


def shards(corr, slope_prev, kappa, detuning, pump, round_trip):
    rows = corr.shape[1]
    cols = corr.shape[2]
    row_start = lax.axis_index("row") * rows
    col_start = lax.axis_index("col") * cols
    kappa_rows = lax.dynamic_slice_in_dim(kappa, row_start, rows)
    kappa_cols = lax.dynamic_slice_in_dim(kappa, col_start, cols)
    detune_rows = lax.dynamic_slice_in_dim(detuning, row_start, rows)
    detune_cols = lax.dynamic_slice_in_dim(detuning, col_start, cols)
    pump_rows = lax.dynamic_slice_in_dim(pump, row_start, rows)
    rho_re = round_trip[0]
    rho_im = round_trip[1]
    section = corr + 0.25 * slope_prev
    upper = section * kappa_rows[None, :, None]
    weighted = section * kappa_cols[None, None, :]
    local_rows, own_rows = rows_prefix(upper)
    local_cols, own_cols = cols_prefix(weighted)
    row_pieces = lax.all_gather(own_rows[None], "row", axis=0, tiled=True)
    dev_rows = lower_devices(row_pieces, lax.axis_index("row"))
    later_rows = higher_devices(row_pieces, lax.axis_index("row"))
    col_pieces = lax.all_gather(own_cols[None], "col", axis=0, tiled=True)
    dev_cols = lower_devices(col_pieces, lax.axis_index("col"))
    later_cols = higher_devices(col_pieces, lax.axis_index("col"))
    before = local_rows + dev_rows[:, None, :]
    after = later_rows[:, None, :] + (own_rows[:, None, :] - local_rows - upper)
    turned = jnp.stack(
        [rho_re * after[0] - rho_im * after[1], rho_re * after[1] + rho_im * after[0]]
    )
    field_left = -kappa_rows[None, :, None] * (before + 0.5 * upper + turned)
    before = local_cols + dev_cols[:, :, None]
    after = later_cols[:, :, None] + (own_cols[:, :, None] - local_cols - weighted)
    turned = jnp.stack(
        [rho_re * after[0] + rho_im * after[1], rho_re * after[1] - rho_im * after[0]]
    )
    field_right = -kappa_cols[None, None, :] * (before + 0.5 * weighted + turned)
    gap = detune_cols[None, :] - detune_rows[:, None]
    spin = jnp.stack([-gap * section[1], gap * section[0]])
    global_rows = row_start + lax.broadcasted_iota(jnp.int32, (rows, cols), 0)
    global_cols = col_start + lax.broadcasted_iota(jnp.int32, (rows, cols), 1)
    source = jnp.where(global_rows == global_cols, pump_rows[:, None], 0.0)
    source = jnp.stack([source, jnp.zeros_like(source)])
    return field_left + field_right + spin + source


def solution(mesh):
    placed = (P(None, "row", "col"), P(None, "row", "col"), P(), P(), P(), P())
    return jax.shard_map(
        shards, mesh=mesh, in_specs=placed, out_specs=P(None, "row", "col"), check_vma=False
    )
```

profile of v0, /device:TPU:0, one launch (start us, length us, event | category | flops | bytes accessed | tf_op | source)
XLA Modules:
  0.0 245.1 jit_solution(6143493666316527245)
XLA Ops:
  0.0 0.7 fusion.18
  0.7 18.0 %fusion.19 = (f32[2,512]{1,0:T(2,128)S(1)}, f32[2,512,4096]{2,1,0:T(8,128)S(1)}, f32[2,512,4096]{2,1,0:T(8,128)}) fusion(f32[4096]{0:T(1024)S(1)} %get-tuple-element.12, f32[2,512,4096]{2,1,0:T(8,128)} %param.6, f32[2,512,4096]{2,1,0:T(8,128)} %param.7), kind=kLoop, calls=%fused_computation.45 | loop fusion | flops 16776192 | bytes 67129344 | tf_op jit(solution)/shard_map/reduce_sum | solution.py:34
  18.7 3.6 %copy.17 = f32[128,8,32,128]{3,2,1,0:T(8,128)S(1)} copy(f32[128,8,32,128]{3,1,2,0:T(8,128)S(1)} %bitcast.42) | data formatting | bytes 33554432
  22.3 2.1 copy-done
  24.4 4.7 %bitcast_reduce_fusion = f32[2,512,32]{2,1,0:T(8,128)S(1)} fusion(f32[2,512,32,128]{3,2,1,0:T(8,128)S(1)} %bitcast.47), kind=kLoop, calls=%fused_computation | loop fusion | flops 4161536 | bytes 16908288 | tf_op jit(solution)/shard_map/reduce_sum | solution.py:32
  29.4 16.1 %broadcast_add_fusion = f32[2,512,32,128]{1,3,2,0:T(8,128)} fusion(f32[2,512,32]{1,2,0:T(8,128)S(1)} %sub.73, f32[2,512,4096]{2,1,0:T(8,128)} %copy-done), kind=kOutput, calls=%fused_computation.24 | convolution fusion | flops 6446661632 | bytes 33685504 | tf_op jit(solution)/shard_map/prbj,ij->prbi/dot_general | solution.py:29
  45.6 17.5 %copy.13 = f32[2,512,4096]{2,1,0:T(8,128)} copy(f32[2,512,4096]{1,2,0:T(8,128)} %bitcast.46) | data formatting | bytes 33554432 | tf_op jit(solution)/shard_map/reshape | solution.py:34
  63.0 5.4 %all-gather.3 = f32[2,2,512]{2,1,0:T(2,128)S(1)} all-gather(f32[1,2,512]{2,1,0:T(2,128)S(1)} %bitcast.49), channel_id=3, replica_groups=mesh['row'=16,'col'=2] {'col'}, dimensions={0}, use_global_device_ids=true | all-gather | bytes 12288 | tf_op jit(solution)/shard_map/all_gather | solution.py:67
  68.6 11.9 %subtract_add_fusion = f32[2,512,4096]{2,1,0:T(8,128)S(1)} fusion(f32[2,512,4096]{2,1,0:T(8,128)} %copy-done, f32[2,512,4096]{2,1,0:T(8,128)} %copy.13, f32[2,512]{1,0:T(2,128)S(1)} %get-tuple-element.13, f32[2,512]{1,0:T(2,128)S(1)} %get-tuple-element.8), kind=kLoop, calls=%fused_computation.16 | loop fusion | flops 12582912 | bytes 50339840 | tf_op jit(solution)/shard_map/add | solution.py:77
  80.5 0.6 fusion.21
  81.2 8.3 %multiply_add_fusion.1 = (f32[1,512,4096]{2,1,0:T(8,128)}, f32[1,512,4096]{2,1,0:T(8,128)}) fusion(f32[2,512,4096]{2,1,0:T(8,128)S(1)} %subtract_add_fusion, f32[]{:T(128)} %bitcast.8, f32[]{:T(128)} %bitcast.6), kind=kLoop, calls=%fused_computation.23 | loop fusion | flops 12582912 | bytes 33554440 | tf_op jit(solution)/shard_map/add | solution.py:79
  89.5 0.8 fusion.17
  90.2 12.0 %fusion.20 = (f32[2,4096]{1,0:T(2,128)S(1)}, f32[2,512,4096]{2,1,0:T(8,128)}) fusion(f32[2,512,4096]{2,1,0:T(8,128)} %get-tuple-element.15, f32[512]{0:T(512)S(1)} %get-tuple-element.10), kind=kLoop, calls=%fused_computation.46 | loop fusion | flops 8380416 | bytes 33589248 | tf_op jit(solution)/shard_map/reduce_sum | solution.py:22
  102.2 7.1 %bitcast_reduce_fusion.1 = f32[2,4,4096]{2,1,0:T(4,128)S(1)} fusion(f32[2,512,4096]{2,1,0:T(8,128)} %get-tuple-element.17), kind=kLoop, calls=%fused_computation.42 | loop fusion | flops 4161536 | bytes 16908288 | tf_op jit(solution)/shard_map/reduce_sum | solution.py:20
  109.4 0.2 reduce_window_sum.22
  109.6 19.5 %convolution_add_fusion = f32[2,4,4096,128]{2,3,1,0:T(8,128)} fusion(f32[2,4,128,4096]{3,2,1,0:T(8,128)} %bitcast.43, f32[2,4,4096]{2,1,0:T(4,128)S(1)} %sub.68), kind=kOutput, calls=%fused_computation.20 | convolution fusion | flops 6446661632 | bytes 33685504 | tf_op jit(solution)/shard_map/ij,pbjc->pbic/dot_general | solution.py:17
  129.1 24.0 %all-gather.2 = f32[16,2,4096]{2,1,0:T(2,128)S(1)} all-gather(f32[1,2,4096]{2,1,0:T(2,128)S(1)} %bitcast.48), channel_id=2, replica_groups=mesh['row'=16,'col'=2] {'row'}, dimensions={0}, use_global_device_ids=true | all-gather | bytes 557056 | tf_op jit(solution)/shard_map/all_gather | solution.py:64
  153.1 0.6 select_reduce_fusion.1
  153.7 18.4 %fusion.10 = f32[2,512,4096]{2,1,0:T(8,128)} fusion(f32[2,512,4096]{2,1,0:T(8,128)} %get-tuple-element.17, f32[2,4,4096,128]{2,3,1,0:T(8,128)} %convolution_add_fusion, f32[2,4096]{1,0:T(2,128)S(1)} %get-tuple-element.16, f32[2,4096]{1,0:T(2,128)S(1)} %get-tuple-element.6), kind=kLoop, calls=%fused_computation.15 | loop fusion | flops 12582912 | bytes 50397184 | tf_op jit(solution)/shard_map/add | solution.py:71
  172.1 13.7 %multiply_subtract_fusion.1 = (f32[1,512,4096]{2,1,0:T(8,128)}, f32[1,512,4096]{2,1,0:T(8,128)}) fusion(f32[2,512,4096]{2,1,0:T(8,128)} %fusion.10, f32[]{:T(128)} %bitcast.8, f32[]{:T(128)} %bitcast.6), kind=kLoop, calls=%fused_computation.27 | loop fusion | flops 12582912 | bytes 33554440 | tf_op jit(solution)/shard_map/sub | solution.py:73
  185.9 6.8 %fusion.11 = (f32[1,512,4096]{2,1,0:T(8,128)}, f32[1,512,4096]{2,1,0:T(8,128)}) fusion(f32[2,512,4096]{2,1,0:T(8,128)S(1)} %bitcast.45, f32[512]{0:T(512)S(1)} %dynamic_slice.18, f32[4096]{0:T(1024)S(1)} %dynamic-slice-done), kind=kLoop, calls=%fused_computation.21 | loop fusion | flops 8388608 | bytes 33572864 | tf_op jit(solution)/shard_map/mul | solution.py:83
  192.7 0.8 dynamic_slice.19
  193.5 4.5 %compare_select_fusion = f32[1,512,4096]{2,1,0:T(8,128)} fusion(f32[512]{0:T(512)S(1)} %dynamic_slice.19, s32[4096]{0:T(1024)S(1)} %iota_add_fusion, s32[512]{0:T(512)S(1)} %iota_add_fusion.1), kind=kLoop, calls=%fused_computation.29 | loop fusion | flops 4194304 | bytes 8409088 | tf_op jit(solution)/shard_map/jit(_where)/select_n | solution.py:86
  198.0 47.1 %fusion.6 = f32[2,512,4096]{2,1,0:T(8,128)} fusion(f32[1,512,4096]{2,1,0:T(8,128)} %get-tuple-element.23, f32[1,512,4096]{2,1,0:T(8,128)} %get-tuple-element.22, f32[1,512,4096]{2,1,0:T(8,128)} %get-tuple-element.21, f32[1,512,4096]{2,1,0:T(8,128)} %get-tuple-element.20, f32[1,512,4096]{2,1,0:T(8,128)} %get-tuple-element.19, ...), kind=kLoop, calls=%fused_computation.8 | loop fusion | flops 67108864 | bytes 142661632 | tf_op jit(solution)/shard_map/add | solution.py:88
  (26 shorter events, 0.6 us)
Async XLA Ops:
  18.7 5.7 %copy-start = (f32[2,512,4096]{2,1,0:T(8,128)}, f32[2,512,4096]{2,1,0:T(8,128)S(1)}, u32[]{:S(2)}) copy-start(f32[2,512,4096]{2,1,0:T(8,128)S(1)} %get-tuple-element.14) | copy-start | bytes 50331652
  68.6 11.9 %copy-start.2 = (f32[2]{0:T(128)S(1)}, f32[2]{0:T(128)}, u32[]{:S(2)}) copy-start(f32[2]{0:T(128)} %param.11) | copy-start | bytes 28
  153.7 32.2 %slice-start = ((s8[16777216]{0:T(1024)(128)(4,1)}), s8[4194304]{0:T(1024)(128)(4,1)S(1)}, s32[]{:S(2)}) async-start(s8[16777216]{0:T(1024)(128)(4,1)} %bitcast.44), calls=%async_computation | async-start | bytes 8388608
  153.7 32.2 %slice-start.1 = ((s8[16777216]{0:T(1024)(128)(4,1)}), s8[4194304]{0:T(1024)(128)(4,1)S(1)}, s32[]{:S(2)}) async-start(s8[16777216]{0:T(1024)(128)(4,1)} %bitcast.44), calls=%async_computation.1 | async-start | bytes 8388608
  153.7 32.2 %slice-start.2 = ((s8[16777216]{0:T(1024)(128)(4,1)}), s8[4194304]{0:T(1024)(128)(4,1)S(1)}, s32[]{:S(2)}) async-start(s8[16777216]{0:T(1024)(128)(4,1)} %bitcast.44), calls=%async_computation.2 | async-start | bytes 8388608
  172.1 13.7 %copy-start.1 = (f32[8192]{0:T(1024)S(1)}, f32[8192]{0:T(1024)}, u32[]{:S(2)}) copy-start(f32[8192]{0:T(1024)} %param.9) | copy-start | bytes 98308
  172.1 13.8 %slice-start.3 = ((s8[16777216]{0:T(1024)(128)(4,1)}), s8[4194304]{0:T(1024)(128)(4,1)S(1)}, s32[]{:S(2)}) async-start(s8[16777216]{0:T(1024)(128)(4,1)} %bitcast.44), calls=%async_computation.3 | async-start | bytes 8388608
  172.1 13.8 %dynamic-slice-start = ((f32[8192]{0:T(1024)}, s32[]{:T(128)}), f32[4096]{0:T(1024)S(1)}, s32[]{:S(2)}) async-start(f32[8192]{0:T(1024)} %param.9, s32[]{:T(128)} %select_n.37), calls=%async_computation.4 | async-start | bytes 33280 | tf_op jit(solution)/shard_map/dynamic_slice | solution.py:55
where the time goes:
time: 246 us; the launch traced here: 245 us
  other arithmetic  155 us (63%)
  matrix products  35.6 us (14%)
  blocking collectives  29.4 us (12%)
  local copies, waits for them, and re-layouts  24.9 us (10%)
    add x1, other arithmetic, shards(): return field_left + field_right + spin + source  47.1 us
    all_gather x1, blocking collectives, shards(): row_pieces = lax.all_gather(own_rows[None], 'row', axis=0, tiled=True)  24 us
    dot_general x1, matrix products, rows_prefix(): jnp.einsum('ij,pbjc->pbic', lower_table(width), blocks, precision=lax.Pre...  19.5 us
    add x1, other arithmetic, shards(): after = later_rows[:, None, :] + (own_rows[:, None, :] - local_rows - upper)  18.4 us
    reduce_sum x1, other arithmetic, cols_prefix(): jnp.sum(sums, axis=2)  18 us
    reshape x1, local copies, waits for them, and re-layouts, cols_prefix(): (within + earlier[:, :, :, None]).reshape(part.shape)  17.5 us
    dot_general x1, matrix products, cols_prefix(): jnp.einsum('prbj,ij->prbi', blocks, lower_table(width), precision=lax.Pre...  16.1 us
    sub x1, other arithmetic, shards(): rho_re * after[0] - rho_im * after[1]  13.7 us

commit v1 on v0

v1 whole, which is shorter than its diff:
```python
import functools

import jax
import jax.numpy as jnp
from jax import lax
from jax.experimental import pallas as pl
from jax.experimental.pallas import tpu as pltpu
from jax.sharding import PartitionSpec as P

WIDTH = 256
SLAB = 32
MESH = pl.DeviceIdType.MESH
VMEM = pl.BlockSpec(memory_space=pltpu.VMEM)
SMEM = pl.BlockSpec(memory_space=pltpu.SMEM)


def split(value):
    high = value.astype(jnp.bfloat16)
    return high, (value - high.astype(jnp.float32)).astype(jnp.bfloat16)


def local_kernel(corr, prev, kappa, detuning, pump, trip, out, row_sums, col_sums,
                 tables, pump_col, u_parts, w_parts, left, right, carry, sums):
    rows = out.shape[1]
    cols = out.shape[2]
    blocks = rows // WIDTH
    step = pl.program_id(0)
    row_start = pl.multiple_of(lax.axis_index("row") * rows, WIDTH)
    col_start = pl.multiple_of(lax.axis_index("col") * cols + step * WIDTH, WIDTH)
    rho_re = trip[0]
    rho_im = trip[1]

    @pl.when(step == 0)
    def _():
        mine = pl.ds(row_start, rows)
        kr = kappa[:, mine]
        stacked = jnp.concatenate(
            [kr, (rho_re - 1.0) * kr, rho_im * kr, (0.5 * rho_re) * kr * kr,
             detuning[:, mine] - (0.5 * rho_im) * kr * kr, pump[:, mine], kr, kr], axis=0)
        columns = jnp.transpose(stacked)
        for n in range(5):
            tables[n] = jnp.broadcast_to(columns[:, n:n + 1], (rows, WIDTH // 2))
        pump_col[...] = jnp.broadcast_to(columns[:, 5:6], (rows, WIDTH // 2))
        carry[...] = jnp.zeros_like(carry)

    here = pl.ds(pl.multiple_of(step * WIDTH, WIDTH), WIDTH)
    kc = kappa[:, pl.ds(col_start, WIDTH)]
    br = (rho_re - 1.0) * kc
    bi = -rho_im * kc
    pk = (0.5 * rho_re) * kc * kc
    ak = detuning[:, pl.ds(col_start, WIDTH)] - (0.5 * rho_im) * kc * kc

    def wide(value):
        return jnp.concatenate([value, value], axis=1)

    above = lax.broadcasted_iota(jnp.int32, (WIDTH, WIDTH), 0)
    beside = lax.broadcasted_iota(jnp.int32, (WIDTH, WIDTH), 1)
    half = jnp.where(above == beside, 0.5, 0.0)
    lower = jnp.where(above > beside, 1.0, half).astype(jnp.bfloat16)
    upper = jnp.where(above < beside, 1.0, half).astype(jnp.bfloat16)
    lower2 = jnp.concatenate([lower, lower], axis=1)
    upper2 = jnp.concatenate([upper, upper], axis=0)

    before = [jnp.zeros((1, WIDTH), jnp.float32)] * 2
    for b in range(blocks):
        def prepare(n, acc):
            low = pl.multiple_of(n * SLAB, SLAB)
            at = pl.ds(pl.multiple_of(b * WIDTH + low, SLAB), SLAB)
            kr = wide(tables[0, at, :])
            new = []
            for p in range(2):
                s = corr[p, at, :] + 0.25 * prev[p, at, :]
                out[p, at, here] = s
                u = s * kr
                high, rest = split(u)
                u_parts[pl.ds(low, SLAB), p * WIDTH:(p + 1) * WIDTH] = high
                u_parts[pl.ds(pl.multiple_of(WIDTH + low, SLAB), SLAB), p * WIDTH:(p + 1) * WIDTH] = rest
                high, rest = split(s * kc)
                w_parts[p, pl.ds(low, SLAB), :WIDTH] = high
                w_parts[p, pl.ds(low, SLAB), WIDTH:] = rest
                new.append(acc[p] + jnp.sum(u.reshape(SLAB // 8, 8, WIDTH), axis=0))
            return tuple(new)

        zero = jnp.zeros((8, WIDTH), jnp.float32)
        acc = lax.fori_loop(0, WIDTH // SLAB, prepare, (zero, zero), unroll=2)

        left[...] = jnp.dot(lower2, u_parts[...], preferred_element_type=jnp.float32)
        for p in range(2):
            right[p] = jnp.dot(w_parts[p], upper2, preferred_element_type=jnp.float32)

        def combine(n, token):
            low = pl.multiple_of(n * SLAB, SLAB)
            at = pl.ds(pl.multiple_of(b * WIDTH + low, SLAB), SLAB)
            near = pl.ds(low, SLAB)
            ar, ai, pi, di = [wide(tables[t, at, :]) for t in range(1, 5)]
            s = [out[p, at, here] for p in range(2)]
            x = [left[near, p * WIDTH:(p + 1) * WIDTH] for p in range(2)]
            if b:
                x = [x[p] + before[p] for p in range(2)]
            y = []
            for p in range(2):
                held = carry[p, at, :]
                piece = right[p, near, :] + wide(held)
                y.append(piece)
                last = piece[:, WIDTH - 1:] + (0.5 * kc[:, WIDTH - 1:]) * s[p][:, WIDTH - 1:]
                carry[p, at, :] = jnp.broadcast_to(last, held.shape)
            cr = pi + pk
            ci = ak - di
            out[0, at, here] = (cr * s[0] - ci * s[1]) + (ar * x[0] - ai * x[1]) + (br * y[0] - bi * y[1])
            out[1, at, here] = (cr * s[1] + ci * s[0]) + (ar * x[1] + ai * x[0]) + (br * y[1] + bi * y[0])
            return token

        lax.fori_loop(0, WIDTH // SLAB, combine, 0, unroll=2)
        before = [before[p] + jnp.sum(acc[p], axis=0, keepdims=True) for p in range(2)]

    offset = col_start - row_start

    @pl.when(jnp.logical_and(offset >= 0, offset < rows))
    def _():
        at = pl.ds(pl.multiple_of(offset, WIDTH), WIDTH)
        out[0, at, here] += jnp.where(above == beside, wide(pump_col[at, :]), 0.0)

    sums[:, here] = jnp.concatenate(before, axis=0)

    @pl.when(step == pl.num_programs(0) - 1)
    def _():
        count, _, width = row_sums.shape
        for n in range(count):
            row_sums[n] = sums[:, n * width:(n + 1) * width]
        for p in range(2):
            col_sums[8 * p:8 * p + 8, :] = jnp.transpose(carry[p])[:8, :]


def prefix_pair(value, total, rho_re, rho_im):
    re = value[0:1] + rho_re * (total[0:1] - value[0:1]) - rho_im * (total[1:2] - value[1:2])
    im = value[1:2] + rho_re * (total[1:2] - value[1:2]) + rho_im * (total[0:1] - value[0:1])
    return re, im


def exchange_kernel(row_sums, col_sums, trip, row_fix, col_fix,
                    got, back, ready, cols_got, send, recv, send_back, recv_back, send_col, recv_col):
    count = row_sums.shape[0]
    col_count = cols_got.shape[0]
    me = lax.axis_index("row")
    my_col = lax.axis_index("col")
    rho_re = trip[0]
    rho_im = trip[1]

    def row_peer(j):
        return (lax.rem(me + j, count), my_col)

    def col_peer(j):
        return (me, lax.rem(my_col + j, col_count))

    barrier = pltpu.get_barrier_semaphore()
    for j in range(1, count):
        pl.semaphore_signal(barrier, inc=1, device_id=row_peer(j), device_id_type=MESH)
    for j in range(1, col_count):
        pl.semaphore_signal(barrier, inc=1, device_id=col_peer(j), device_id_type=MESH)
    pl.semaphore_wait(barrier, count + col_count - 2)

    first, second, across = [], [], []
    for j in range(1, count):
        first.append(pltpu.make_async_remote_copy(
            src_ref=row_sums.at[lax.rem(me + j, count)], dst_ref=got.at[j],
            send_sem=send.at[j], recv_sem=recv.at[j], device_id=row_peer(j), device_id_type=MESH))
        first[-1].start()
    for j in range(1, col_count):
        across.append(pltpu.make_async_remote_copy(
            src_ref=col_sums, dst_ref=cols_got.at[j],
            send_sem=send_col.at[j], recv_sem=recv_col.at[j], device_id=col_peer(j), device_id_type=MESH))
        across[-1].start()
    got[0] = row_sums[me]
    cols_got[0] = col_sums[...]
    for copy in first:
        copy.wait_recv()
    running = jnp.zeros(got.shape[1:], jnp.float32)
    held = []
    for n in range(count):
        held.append(running)
        running = running + got[lax.rem(me - n + count, count)]
    for n in range(count):
        re, im = prefix_pair(held[n], running, rho_re, rho_im)
        ready[lax.rem(n - me + count, count)] = jnp.concatenate([re, im], axis=0)
    for j in range(1, count):
        second.append(pltpu.make_async_remote_copy(
            src_ref=ready.at[j], dst_ref=back.at[j],
            send_sem=send_back.at[j], recv_sem=recv_back.at[j], device_id=row_peer(j), device_id_type=MESH))
        second[-1].start()
    for copy in across:
        copy.wait_recv()
    running = jnp.zeros(col_sums.shape, jnp.float32)
    mine = running
    for n in range(col_count):
        piece = cols_got[lax.rem(my_col - n + col_count, col_count)]
        mine = mine + jnp.where(n < my_col, piece, 0.0)
        running = running + piece
    rest = running - mine
    col_fix[0:8, :] = mine[0:8] + rho_re * rest[0:8] + rho_im * rest[8:16]
    col_fix[8:16, :] = mine[8:16] + rho_re * rest[8:16] - rho_im * rest[0:8]
    for copy in second:
        copy.wait_recv()
    row_fix[me] = ready[0]
    for j in range(1, count):
        row_fix[lax.rem(me - j + count, count)] = back[j]
    for copy in first + across + second:
        copy.wait_send()


def finish_kernel(local, row_fix, col_fix, kappa, out, tables, across):
    step = pl.program_id(0)
    rows = local.shape[1]
    cols = local.shape[2]
    slab = out.shape[1]

    @pl.when(step == 0)
    def _():
        mine = pl.ds(pl.multiple_of(lax.axis_index("row") * rows, WIDTH), rows)
        stacked = jnp.concatenate([col_fix[0:1, :], col_fix[8:9, :], kappa[:, mine]] + [col_fix[0:5, :]], axis=0)
        columns = jnp.transpose(stacked)
        for n in range(3):
            tables[n] = jnp.broadcast_to(columns[:, n:n + 1], tables.shape[1:])
        count = row_fix.shape[0]
        across[...] = jnp.concatenate([row_fix[n] for n in range(count)], axis=1)

    at = pl.ds(pl.multiple_of(step * slab, slab), slab)
    col_start = lax.axis_index("col") * cols
    kr = tables[2, at, :]
    fix = [tables[p, at, :] for p in range(2)]
    for n in range(cols // 128):
        here = slice(n * 128, (n + 1) * 128)
        kc = kappa[:, pl.ds(pl.multiple_of(col_start + n * 128, 128), 128)]
        for p in range(2):
            out[p, :, here] = local[p, at, here] - kr * across[p:p + 1, here] - kc * fix[p]


def shards(row_count, col_count, corr, slope_prev, kappa, detuning, pump, round_trip):
    _, rows, cols = corr.shape
    width = cols // row_count
    kappa, detuning, pump = [v.reshape(1, -1) for v in (kappa, detuning, pump)]
    f32 = jnp.float32
    block = pl.BlockSpec((2, rows, WIDTH), lambda c: (0, 0, c))
    local, row_sums, col_sums = pl.pallas_call(
        local_kernel,
        grid=(cols // WIDTH,),
        out_shape=(
            pltpu.VMEM((2, rows, cols), f32),
            jax.ShapeDtypeStruct((row_count, 2, width), f32),
            jax.ShapeDtypeStruct((16, rows), f32),
        ),
        in_specs=[block, block, VMEM, VMEM, VMEM, SMEM],
        out_specs=(VMEM, VMEM, VMEM),
        scratch_shapes=[
            pltpu.VMEM((5, rows, WIDTH // 2), f32),
            pltpu.VMEM((rows, WIDTH // 2), f32),
            pltpu.VMEM((2 * WIDTH, 2 * WIDTH), jnp.bfloat16),
            pltpu.VMEM((2, WIDTH, 2 * WIDTH), jnp.bfloat16),
            pltpu.VMEM((WIDTH, 2 * WIDTH), f32),
            pltpu.VMEM((2, WIDTH, WIDTH), f32),
            pltpu.VMEM((2, rows, WIDTH // 2), f32),
            pltpu.VMEM((2, cols), f32),
        ],
        compiler_params=pltpu.CompilerParams(vmem_limit_bytes=34 << 20),
        name="local_part",
    )(corr, slope_prev, kappa, detuning, pump, round_trip)
    piece = (row_count, 2, width)
    row_fix, col_fix = pl.pallas_call(
        exchange_kernel,
        out_shape=(jax.ShapeDtypeStruct(piece, f32), jax.ShapeDtypeStruct((16, rows), f32)),
        in_specs=[VMEM, VMEM, SMEM],
        out_specs=(VMEM, VMEM),
        scratch_shapes=[
            pltpu.VMEM(piece, f32),
            pltpu.VMEM(piece, f32),
            pltpu.VMEM(piece, f32),
            pltpu.VMEM((col_count, 16, rows), f32),
        ] + [pltpu.SemaphoreType.DMA((row_count,))] * 4 + [pltpu.SemaphoreType.DMA((col_count,))] * 2,
        compiler_params=pltpu.CompilerParams(
            collective_id=0, has_side_effects=True, vmem_limit_bytes=6 << 20),
        name="exchange_sums",
    )(row_sums, col_sums, round_trip)
    slab = 32
    return pl.pallas_call(
        finish_kernel,
        grid=(rows // slab,),
        out_shape=jax.ShapeDtypeStruct((2, rows, cols), f32),
        in_specs=[VMEM, VMEM, VMEM, VMEM],
        out_specs=pl.BlockSpec((2, slab, cols), lambda r: (0, r, 0)),
        scratch_shapes=[pltpu.VMEM((3, rows, 128), f32), pltpu.VMEM((2, cols), f32)],
        compiler_params=pltpu.CompilerParams(vmem_limit_bytes=10 << 20),
        name="finish",
    )(local, row_fix, col_fix, kappa)


def solution(mesh):
    placed = (P(None, "row", "col"), P(None, "row", "col"), P(), P(), P(), P())
    body = functools.partial(shards, mesh.shape["row"], mesh.shape["col"])
    return jax.shard_map(
        body, mesh=mesh, in_specs=placed, out_specs=P(None, "row", "col"), check_vma=False
    )
```

time: 246 us -> 86.8 us (0.35)
  other arithmetic: 155 us -> 0 us
  Pallas kernels: 0 us -> 83.5 us
  matrix products: 35.6 us -> 0 us
  blocking collectives: 29.4 us -> 0 us
  local copies, waits for them, and re-layouts: 24.9 us -> 2.93 us
    add x6 -> x0, other arithmetic: 85.7 us -> none  [the longest x1 47.1 us: shards(): return field_left + field_right + spin + source]
    pallas_call x0 -> x3, Pallas kernels: none -> 83.5 us  [the longest x1 58.5 us: shards(): pl.pallas_call(local_kernel, grid=(cols // WIDTH,), out_shape=(pltpu.VMEM...]
    reduce_sum x6 -> x0, other arithmetic: 42.5 us -> none  [the longest x1 18 us: cols_prefix(): jnp.sum(sums, axis=2)]
    dot_general x2 -> x0, matrix products: 35.6 us -> none  [the longest x1 19.5 us: rows_prefix(): jnp.einsum('ij,pbjc->pbic', lower_table(width), blocks, precision=lax.Pre...]
    all_gather x2 -> x0, blocking collectives: 29.4 us -> none  [the longest x1 24 us: shards(): row_pieces = lax.all_gather(own_rows[None], 'row', axis=0, tiled=True)]
    reshape x1 -> x0, local copies, waits for them, and re-layouts: 17.5 us -> none  [cols_prefix(): (within + earlier[:, :, :, None]).reshape(part.shape)]
    sub x3 -> x0, other arithmetic: 13.8 us -> none  [the longest x1 13.7 us: shards(): rho_re * after[0] - rho_im * after[1]]
    mul x1 -> x0, other arithmetic: 6.82 us -> none  [shards(): spin = jnp.stack([-gap * section[1], gap * section[0]])]
where the time goes in v1:
time: 86.8 us; the launch traced here: 86.5 us
  Pallas kernels  83.5 us (96%)
  local copies, waits for them, and re-layouts  2.93 us (3%)
    pallas_call x1, Pallas kernels, shards(): pl.pallas_call(local_kernel, grid=(cols // WIDTH,), out_shape=(pltpu.VMEM...  58.5 us
    pallas_call x1, Pallas kernels, shards(): pl.pallas_call(exchange_kernel, out_shape=(jax.ShapeDtypeStruct(piece, f3...  15.3 us
    pallas_call x1, Pallas kernels, shards(): pl.pallas_call(finish_kernel, grid=(rows // slab,), out_shape=jax.ShapeDt...  9.8 us
    unnamed x8, local copies, waits for them, and re-layouts  2.93 us

profile of v1, /device:TPU:0, one launch (start us, length us, event | category | flops | bytes accessed | tf_op | source)
XLA Modules:
  0.0 86.5 jit_solution(1644296154859214401)
XLA Ops:
  0.0 0.0 copy-start
  0.0 0.8 copy-done
  0.8 0.0 copy-start.1
  0.8 0.8 copy-done.1
  1.5 0.0 copy-start.2
  1.5 0.8 copy-done.2
  2.3 0.0 copy-start.3
  2.3 0.7 copy-done.3
  2.9 58.5 %local_part.1 = (f32[2,512,4096]{2,1,0:T(8,128)S(1)}, f32[16,2,256]{2,1,0:T(2,128)S(1)}, f32[16,512]{1,0:T(8,128)S(1)}) custom-call(f32[2,512,4096]{2,1,0:T(8,128)} %corr.1, f32[2,512,4096]{2,1,0:T(8,128)} %prev.1, f32[1,8192]{1,0:T(1,128)S(1)} %bitcast.3, f32[1,8192]{1,0:T(1,128)S(1)} %bitcast.5, f32[1,8192]{1,0:T(1,128)S(1)} %bitcast.6, f32[2]{0:T(128)S(1)} %copy-done.3), custom_call_target="tpu_custom_call" | custom-call | tf_op jit(solution)/shard_map/local_part/pallas_call | solution.py:243
  61.4 15.3 %exchange_sums.1 = (f32[16,2,256]{2,1,0:T(2,128)S(1)}, f32[16,512]{1,0:T(8,128)S(1)}) custom-call(f32[16,2,256]{2,1,0:T(2,128)S(1)} %get-tuple-element.11.row_sums, f32[16,512]{1,0:T(8,128)S(1)} %get-tuple-element.12.col_sums, f32[2]{0:T(128)S(1)} %copy-done.3), custom_call_target="tpu_custom_call" | custom-call | tf_op jit(solution)/shard_map/exchange_sums/pallas_call | solution.py:267
  76.7 9.8 %finish.1 = f32[2,512,4096]{2,1,0:T(8,128)} custom-call(f32[2,512,4096]{2,1,0:T(8,128)S(1)} %get-tuple-element.10.local, f32[16,2,256]{2,1,0:T(2,128)S(1)} %get-tuple-element.13.row_fix, f32[16,512]{1,0:T(8,128)S(1)} %get-tuple-element.14.col_fix, f32[1,8192]{1,0:T(1,128)S(1)} %bitcast.4), custom_call_target="tpu_custom_call" | custom-call | tf_op jit(solution)/shard_map/finish/pallas_call | solution.py:283
Async XLA Ops:
  0.0 0.8 copy-start
  0.8 0.8 copy-start.1
  1.5 0.8 copy-start.2
  2.3 0.7 copy-start.3

commit v2 on v1

--- a/solution.py
+++ b/solution.py
@@ -8,7 +8,8 @@
 from jax.sharding import PartitionSpec as P
 
 WIDTH = 256
-SLAB = 32
+TRI = 128
+SLAB = 16
 MESH = pl.DeviceIdType.MESH
 VMEM = pl.BlockSpec(memory_space=pltpu.VMEM)
 SMEM = pl.BlockSpec(memory_space=pltpu.SMEM)
@@ -20,10 +21,10 @@
 
 
 def local_kernel(corr, prev, kappa, detuning, pump, trip, out, row_sums, col_sums,
-                 tables, pump_col, u_parts, w_parts, left, right, carry, sums):
+                 tables, pump_col, u_parts, w_parts, left, right, carry, sums, lower2, upper2, section):
     rows = out.shape[1]
     cols = out.shape[2]
-    blocks = rows // WIDTH
+    blocks = rows // TRI
     step = pl.program_id(0)
     row_start = pl.multiple_of(lax.axis_index("row") * rows, WIDTH)
     col_start = pl.multiple_of(lax.axis_index("col") * cols + step * WIDTH, WIDTH)
@@ -42,6 +43,14 @@
             tables[n] = jnp.broadcast_to(columns[:, n:n + 1], (rows, WIDTH // 2))
         pump_col[...] = jnp.broadcast_to(columns[:, 5:6], (rows, WIDTH // 2))
         carry[...] = jnp.zeros_like(carry)
+        above = lax.broadcasted_iota(jnp.int32, (TRI, TRI), 0)
+        beside = lax.broadcasted_iota(jnp.int32, (TRI, TRI), 1)
+        half = jnp.where(above == beside, 0.5, 0.0)
+        lower = jnp.where(above > beside, 1.0, half).astype(jnp.bfloat16)
+        upper = jnp.where(above < beside, 1.0, half).astype(jnp.bfloat16)
+        full = jnp.ones((2 * TRI, TRI), jnp.bfloat16)
+        lower2[...] = jnp.concatenate([lower, lower], axis=1)
+        upper2[...] = jnp.concatenate([jnp.concatenate([upper, upper], axis=0), full], axis=1)
 
     here = pl.ds(pl.multiple_of(step * WIDTH, WIDTH), WIDTH)
     kc = kappa[:, pl.ds(col_start, WIDTH)]
@@ -53,71 +62,62 @@
     def wide(value):
         return jnp.concatenate([value, value], axis=1)
 
-    above = lax.broadcasted_iota(jnp.int32, (WIDTH, WIDTH), 0)
-    beside = lax.broadcasted_iota(jnp.int32, (WIDTH, WIDTH), 1)
-    half = jnp.where(above == beside, 0.5, 0.0)
-    lower = jnp.where(above > beside, 1.0, half).astype(jnp.bfloat16)
-    upper = jnp.where(above < beside, 1.0, half).astype(jnp.bfloat16)
-    lower2 = jnp.concatenate([lower, lower], axis=1)
-    upper2 = jnp.concatenate([upper, upper], axis=0)
-
-    before = [jnp.zeros((1, WIDTH), jnp.float32)] * 2
+    before = [[jnp.zeros((1, WIDTH), jnp.float32)] * 2]
     for b in range(blocks):
-        def prepare(n, acc):
-            low = pl.multiple_of(n * SLAB, SLAB)
-            at = pl.ds(pl.multiple_of(b * WIDTH + low, SLAB), SLAB)
+        acc = [jnp.zeros((8, WIDTH), jnp.float32)] * 2
+        for low in range(0, TRI, SLAB):
+            at = slice(b * TRI + low, b * TRI + low + SLAB)
             kr = wide(tables[0, at, :])
-            new = []
             for p in range(2):
+                lanes = slice(p * WIDTH, (p + 1) * WIDTH)
                 s = corr[p, at, :] + 0.25 * prev[p, at, :]
-                out[p, at, here] = s
+                section[p, at, :] = s
                 u = s * kr
                 high, rest = split(u)
-                u_parts[pl.ds(low, SLAB), p * WIDTH:(p + 1) * WIDTH] = high
-                u_parts[pl.ds(pl.multiple_of(WIDTH + low, SLAB), SLAB), p * WIDTH:(p + 1) * WIDTH] = rest
+                u_parts[b, low:low + SLAB, lanes] = high
+                u_parts[b, TRI + low:TRI + low + SLAB, lanes] = rest
                 high, rest = split(s * kc)
-                w_parts[p, pl.ds(low, SLAB), :WIDTH] = high
-                w_parts[p, pl.ds(low, SLAB), WIDTH:] = rest
-                new.append(acc[p] + jnp.sum(u.reshape(SLAB // 8, 8, WIDTH), axis=0))
-            return tuple(new)
-
-        zero = jnp.zeros((8, WIDTH), jnp.float32)
-        acc = lax.fori_loop(0, WIDTH // SLAB, prepare, (zero, zero), unroll=2)
-
-        left[...] = jnp.dot(lower2, u_parts[...], preferred_element_type=jnp.float32)
-        for p in range(2):
-            right[p] = jnp.dot(w_parts[p], upper2, preferred_element_type=jnp.float32)
-
-        def combine(n, token):
-            low = pl.multiple_of(n * SLAB, SLAB)
-            at = pl.ds(pl.multiple_of(b * WIDTH + low, SLAB), SLAB)
-            near = pl.ds(low, SLAB)
+                for c in range(WIDTH // TRI):
+                    beneath = slice(c * TRI, (c + 1) * TRI)
+                    w_parts[b, c, p * TRI + low:p * TRI + low + SLAB, :TRI] = high[:, beneath]
+                    w_parts[b, c, p * TRI + low:p * TRI + low + SLAB, TRI:] = rest[:, beneath]
+                acc[p] = acc[p] + jnp.sum(u.reshape(SLAB // 8, 8, WIDTH), axis=0)
+        left[b] = jnp.dot(lower2[...], u_parts[b], preferred_element_type=jnp.float32)
+        for c in range(WIDTH // TRI):
+            right[b, c] = jnp.dot(w_parts[b, c], upper2[...], preferred_element_type=jnp.float32)
+        before.append([before[-1][p] + jnp.sum(acc[p], axis=0, keepdims=True) for p in range(2)])
+
+    for b in range(blocks):
+        for low in range(0, TRI, SLAB):
+            at = slice(b * TRI + low, b * TRI + low + SLAB)
             ar, ai, pi, di = [wide(tables[t, at, :]) for t in range(1, 5)]
-            s = [out[p, at, here] for p in range(2)]
-            x = [left[near, p * WIDTH:(p + 1) * WIDTH] for p in range(2)]
+            s = [section[p, at, :] for p in range(2)]
+            x = [left[b, low:low + SLAB, p * WIDTH:(p + 1) * WIDTH] for p in range(2)]
             if b:
-                x = [x[p] + before[p] for p in range(2)]
+                x = [x[p] + before[b][p] for p in range(2)]
             y = []
             for p in range(2):
                 held = carry[p, at, :]
-                piece = right[p, near, :] + wide(held)
-                y.append(piece)
-                last = piece[:, WIDTH - 1:] + (0.5 * kc[:, WIDTH - 1:]) * s[p][:, WIDTH - 1:]
-                carry[p, at, :] = jnp.broadcast_to(last, held.shape)
+                near = slice(p * TRI + low, p * TRI + low + SLAB)
+                pieces = []
+                for c in range(WIDTH // TRI):
+                    pieces.append(right[b, c, near, :TRI] + held)
+                    held = held + right[b, c, near, TRI:]
+                y.append(jnp.concatenate(pieces, axis=1))
+                carry[p, at, :] = held
             cr = pi + pk
             ci = ak - di
             out[0, at, here] = (cr * s[0] - ci * s[1]) + (ar * x[0] - ai * x[1]) + (br * y[0] - bi * y[1])
             out[1, at, here] = (cr * s[1] + ci * s[0]) + (ar * x[1] + ai * x[0]) + (br * y[1] + bi * y[0])
-            return token
-
-        lax.fori_loop(0, WIDTH // SLAB, combine, 0, unroll=2)
-        before = [before[p] + jnp.sum(acc[p], axis=0, keepdims=True) for p in range(2)]
+    before = before[-1]
 
     offset = col_start - row_start
 
     @pl.when(jnp.logical_and(offset >= 0, offset < rows))
     def _():
         at = pl.ds(pl.multiple_of(offset, WIDTH), WIDTH)
+        above = lax.broadcasted_iota(jnp.int32, (WIDTH, WIDTH), 0)
+        beside = lax.broadcasted_iota(jnp.int32, (WIDTH, WIDTH), 1)
         out[0, at, here] += jnp.where(above == beside, wide(pump_col[at, :]), 0.0)
 
     sums[:, here] = jnp.concatenate(before, axis=0)
@@ -253,12 +253,15 @@
         scratch_shapes=[
             pltpu.VMEM((5, rows, WIDTH // 2), f32),
             pltpu.VMEM((rows, WIDTH // 2), f32),
-            pltpu.VMEM((2 * WIDTH, 2 * WIDTH), jnp.bfloat16),
-            pltpu.VMEM((2, WIDTH, 2 * WIDTH), jnp.bfloat16),
-            pltpu.VMEM((WIDTH, 2 * WIDTH), f32),
-            pltpu.VMEM((2, WIDTH, WIDTH), f32),
+            pltpu.VMEM((rows // TRI, 2 * TRI, 2 * WIDTH), jnp.bfloat16),
+            pltpu.VMEM((rows // TRI, WIDTH // TRI, 2 * TRI, 2 * TRI), jnp.bfloat16),
+            pltpu.VMEM((rows // TRI, TRI, 2 * WIDTH), f32),
+            pltpu.VMEM((rows // TRI, WIDTH // TRI, 2 * TRI, 2 * TRI), f32),
             pltpu.VMEM((2, rows, WIDTH // 2), f32),
             pltpu.VMEM((2, cols), f32),
+            pltpu.VMEM((TRI, 2 * TRI), jnp.bfloat16),
+            pltpu.VMEM((2 * TRI, 2 * TRI), jnp.bfloat16),
+            pltpu.VMEM((2, rows, WIDTH), f32),
         ],
         compiler_params=pltpu.CompilerParams(vmem_limit_bytes=34 << 20),
         name="local_part",

time: 86.8 us -> 52.3 us (0.60)
  Pallas kernels: 83.5 us -> 48.7 us
    pallas_call x1, Pallas kernels: 58.5 us -> 23.5 us  [shards(): pl.pallas_call(local_kernel, grid=(cols // WIDTH,), out_shape=(pltpu.VMEM...]
where the time goes in v2:
time: 52.3 us; the launch traced here: 51.6 us
  Pallas kernels  48.7 us (93%)
  local copies, waits for them, and re-layouts  2.93 us (6%)
    pallas_call x1, Pallas kernels, shards(): pl.pallas_call(local_kernel, grid=(cols // WIDTH,), out_shape=(pltpu.VMEM...  23.5 us
    pallas_call x1, Pallas kernels, shards(): pl.pallas_call(exchange_kernel, out_shape=(jax.ShapeDtypeStruct(piece, f3...  15.3 us
    pallas_call x1, Pallas kernels, shards(): pl.pallas_call(finish_kernel, grid=(rows // slab,), out_shape=jax.ShapeDt...  9.8 us
    unnamed x8, local copies, waits for them, and re-layouts  2.93 us

profile of v2, /device:TPU:0, one launch (start us, length us, event | category | flops | bytes accessed | tf_op | source)
XLA Modules:
  0.0 51.6 jit_solution(6987186948486161036)
XLA Ops:
  0.0 0.0 copy-start
  0.0 0.8 %copy-done = f32[8192]{0:T(1024)S(1)} copy-done((f32[8192]{0:T(1024)S(1)}, f32[8192]{0:T(1024)}, u32[]{:S(2)}) %copy-start) | copy-done | bytes 32792
  0.8 0.0 copy-start.1
  0.8 0.8 %copy-done.1 = f32[8192]{0:T(1024)S(1)} copy-done((f32[8192]{0:T(1024)S(1)}, f32[8192]{0:T(1024)}, u32[]{:S(2)}) %copy-start.1) | copy-done | bytes 32792
  1.5 0.0 copy-start.2
  1.5 0.8 %copy-done.2 = f32[8192]{0:T(1024)S(1)} copy-done((f32[8192]{0:T(1024)S(1)}, f32[8192]{0:T(1024)}, u32[]{:S(2)}) %copy-start.2) | copy-done | bytes 32792
  2.3 0.0 copy-start.3
  2.3 0.7 %copy-done.3 = f32[2]{0:T(128)S(1)} copy-done((f32[2]{0:T(128)S(1)}, f32[2]{0:T(128)}, u32[]{:S(2)}) %copy-start.3) | copy-done | bytes 32
  2.9 23.5 %local_part.1 = (f32[2,512,4096]{2,1,0:T(8,128)S(1)}, f32[16,2,256]{2,1,0:T(2,128)S(1)}, f32[16,512]{1,0:T(8,128)S(1)}) custom-call(f32[2,512,4096]{2,1,0:T(8,128)} %corr.1, f32[2,512,4096]{2,1,0:T(8,128)} %prev.1, f32[1,8192]{1,0:T(1,128)S(1)} %bitcast.3, f32[1,8192]{1,0:T(1,128)S(1)} %bitcast.5, f32[1,8192]{1,0:T(1,128)S(1)} %bitcast.6, f32[2]{0:T(128)S(1)} %copy-done.3), custom_call_target="tpu_custom_call" | custom-call | tf_op jit(solution)/shard_map/local_part/pallas_call | solution.py:243
  26.5 15.3 %exchange_sums.1 = (f32[16,2,256]{2,1,0:T(2,128)S(1)}, f32[16,512]{1,0:T(8,128)S(1)}) custom-call(f32[16,2,256]{2,1,0:T(2,128)S(1)} %get-tuple-element.11.row_sums, f32[16,512]{1,0:T(8,128)S(1)} %get-tuple-element.12.col_sums, f32[2]{0:T(128)S(1)} %copy-done.3), custom_call_target="tpu_custom_call" | custom-call | tf_op jit(solution)/shard_map/exchange_sums/pallas_call | solution.py:270
  41.8 9.8 %finish.1 = f32[2,512,4096]{2,1,0:T(8,128)} custom-call(f32[2,512,4096]{2,1,0:T(8,128)S(1)} %get-tuple-element.10.local, f32[16,2,256]{2,1,0:T(2,128)S(1)} %get-tuple-element.13.row_fix, f32[16,512]{1,0:T(8,128)S(1)} %get-tuple-element.14.col_fix, f32[1,8192]{1,0:T(1,128)S(1)} %bitcast.4), custom_call_target="tpu_custom_call" | custom-call | tf_op jit(solution)/shard_map/finish/pallas_call | solution.py:286
Async XLA Ops:
  0.0 0.8 %copy-start = (f32[8192]{0:T(1024)S(1)}, f32[8192]{0:T(1024)}, u32[]{:S(2)}) copy-start(f32[8192]{0:T(1024)} %param.8) | copy-start | bytes 98308
  0.8 0.8 %copy-start.1 = (f32[8192]{0:T(1024)S(1)}, f32[8192]{0:T(1024)}, u32[]{:S(2)}) copy-start(f32[8192]{0:T(1024)} %param.9) | copy-start | bytes 98308
  1.5 0.8 %copy-start.2 = (f32[8192]{0:T(1024)S(1)}, f32[8192]{0:T(1024)}, u32[]{:S(2)}) copy-start(f32[8192]{0:T(1024)} %param.10) | copy-start | bytes 98308
  2.3 0.7 %copy-start.3 = (f32[2]{0:T(128)S(1)}, f32[2]{0:T(128)}, u32[]{:S(2)}) copy-start(f32[2]{0:T(128)} %trip.3) | copy-start | bytes 28
